TPU v7x, 32 devices: a whole 2x2x4 slice. The times are simulated.
32 devices in a mesh: slab: 4 (over y, x), row: 4 (over z), col: 2 (over core).
Axes of the slice: x: 2, y: 2, z: 4, core: 2. Of those that a mesh axis runs over, the one named last changes fastest.
Arguments:
- wave: float32 [16, 32, 32, 256], P(None, 'slab', 'row', 'col')
- potential: float32 [32, 32, 256], P('slab', 'row', 'col'), may hold values from -1 to 1
- positions: int32 [3, 256], P(None, ('slab', 'row', 'col')), may hold values from 0 to 255, as said below
- species: int32 [256], P(('slab', 'row', 'col')), may hold values from 0 to 3
- counts: int32 [32], P(('slab', 'row', 'col')), may hold values from 1 to 8, as said below
- offsets: int32 [4, 3, 384], replicated, may hold values from -5 to 5, as said below
- beta: float32 [4, 384], replicated, may hold values from -0.3125 to 0.3125
- coupling: float32 [4], replicated, may hold values from 0.5 to 4
Outputs:
- filtered: float32 [16, 32, 32, 256], P(None, 'slab', 'row', 'col')
- gram: float32 [16, 16], replicated
Inputs may be any that keep to these rules, and one draw needn't show every extreme that they name: `positions`: slot j belongs to block j // 8, blocks numbered with the first dimension slowest and the third fastest; its position lies inside that block of 8 x 8 x 128 cells; the first slot sits at the grid's first cell and the last slot at its last cell. `counts`: some block has all 8 slots live. `offsets`: each species' points are distinct lattice points at distance 5 or less from the anchor, and include the six points at distance 5 along the axes.
All inputs are finite; a program needn't handle non-finite values.
Results may differ from a plain program's by a relative error of at most 0.000086.
Values sent between devices are 32-bit elements; how exact they have to be, the bound alone decides.
A program may use at most 192 MiB of HBM per device.

v0:
```python
import jax
import jax.numpy as jnp
import ml_dtypes
import numpy as np
from jax import lax
from jax.experimental import pallas as pl
from jax.experimental.pallas import tpu as pltpu
from jax.sharding import PartitionSpec as P

stencil_weights = (
    -5369.0 / 1800.0,
    12.0 / 7.0,
    -15.0 / 56.0,
    10.0 / 189.0,
    -1.0 / 112.0,
    2.0 / 1925.0,
    -1.0 / 16632.0,
)
lower_edge = 3.0
upper_edge = 17.0


def padded_2(block, sides, width):
    for axis, dim in sides:
        count = lax.axis_size(axis)
        forward = [(i, i + 1) for i in range(count - 1)]
        backward = [(target, source) for source, target in forward]
        low = lax.ppermute(
            lax.slice_in_dim(block, block.shape[dim] - width, None, axis=dim), axis, forward
        )
        high = lax.ppermute(lax.slice_in_dim(block, 0, width, axis=dim), axis, backward)
        block = jnp.concatenate([low, block, high], axis=dim)
    return block


def stencil(padded, extent):
    size_x, size_y, size_z = extent

    def window(shift_x, shift_y, shift_z):
        return padded[
            :,
            6 + shift_x : 6 + shift_x + size_x,
            6 + shift_y : 6 + shift_y + size_y,
            6 + shift_z : 6 + shift_z + size_z,
        ]

    total = 3.0 * stencil_weights[0] * window(0, 0, 0)
    for reach in range(1, 7):
        paired = (
            window(reach, 0, 0)
            + window(-reach, 0, 0)
            + window(0, reach, 0)
            + window(0, -reach, 0)
            + window(0, 0, reach)
            + window(0, 0, -reach)
        )
        total = total + stencil_weights[reach] * paired
    return total


def atom_tables(species, offsets, beta, coupling):
    matches = species[:, None] == jnp.arange(beta.shape[0], dtype=jnp.int32)[None]
    onehot = matches.astype(jnp.float32)
    shapes = jnp.dot(onehot, beta, precision=lax.Precision.HIGHEST)
    gains = jnp.sum(onehot * coupling[None], axis=1)
    offset_rows = jnp.sum(jnp.where(matches[:, :, None, None], offsets[None], 0), axis=1)
    return (shapes, offset_rows, gains)


def add_rims(accumulated, received, axis_dim):
    length = accumulated.shape[axis_dim]
    inner = lax.slice_in_dim(accumulated, 6, length - 6, axis=axis_dim)
    lower_part = lax.slice_in_dim(received, 0, 6, axis=axis_dim)
    upper_part = lax.slice_in_dim(received, 18, 24, axis=axis_dim)
    leading = [slice(None)] * 4
    leading[axis_dim] = slice(0, 6)
    inner = inner.at[tuple(leading)].add(lower_part)
    trailing = [slice(None)] * 4
    trailing[axis_dim] = slice(length - 18, length - 12)
    return inner.at[tuple(trailing)].add(upper_part)


def shards(wave, potential, positions, species, counts, offsets, beta, coupling):
    bands, size_x, size_y, size_z = wave.shape
    extent = (size_x, size_y, size_z)
    wide_x, wide_y, wide_z = (size_x + 12, size_y + 12, size_z + 12)
    anchor = jnp.stack(
        [
            lax.axis_index("slab") * size_x,
            lax.axis_index("row") * size_y,
            lax.axis_index("col") * size_z,
        ]
    )
    slot_count = positions.shape[1]
    own_shapes, own_offsets, own_gains = atom_tables(species, offsets, beta, coupling)
    active = (jnp.arange(slot_count, dtype=jnp.int32) < counts[0]).astype(jnp.float32)
    own_weights = own_gains * active
    local = positions.T[:, :, None] - anchor[None, :, None] + own_offsets + 6
    ext_index = ((local[:, 0] * wide_y + local[:, 1]) * wide_z + local[:, 2]).reshape(-1)
    centre = 0.5 * (upper_edge + lower_edge)
    half_width = 0.5 * (upper_edge - lower_edge)

    def spread_rims(scaled):
        contributions = (scaled[:, :, None] * own_shapes[None]).reshape(bands, -1)
        accumulated = (
            jnp.zeros((bands, wide_x * wide_y * wide_z), jnp.float32)
            .at[:, ext_index]
            .add(contributions)
        )
        accumulated = accumulated.reshape(bands, wide_x, wide_y, wide_z)
        rims = jnp.concatenate([accumulated[:, :6], accumulated[:, -6:]], axis=1)
        received = padded_2(rims, (("slab", 1),), 6)
        accumulated = add_rims(accumulated, received, 1)
        rims = jnp.concatenate([accumulated[:, :, :6], accumulated[:, :, -6:]], axis=2)
        received = padded_2(rims, (("row", 2),), 6)
        accumulated = add_rims(accumulated, received, 2)
        rims = jnp.concatenate([accumulated[:, :, :, :6], accumulated[:, :, :, -6:]], axis=3)
        received = padded_2(rims, (("col", 3),), 6)
        return add_rims(accumulated, received, 3)

    def filter_step(field):
        padded = padded_2(field, (("slab", 1), ("row", 2), ("col", 3)), 6)
        picked = jnp.take(padded.reshape(bands, -1), ext_index, axis=1).reshape(
            bands, slot_count, -1
        )
        projected = jnp.sum(picked * own_shapes[None], axis=2)
        scaled = projected * own_weights[None]
        projector_part = spread_rims(scaled)
        applied = -0.5 * stencil(padded, extent) + potential[None] * field + projector_part
        return (applied - centre * field) / half_width

    first = filter_step(wave)
    second = 2.0 * filter_step(first) - wave
    third = 2.0 * filter_step(second) - first
    flattened = third.reshape(bands, -1)
    partial_gram = jnp.dot(flattened, flattened.T, precision=lax.Precision.HIGHEST)
    summed_gram = lax.psum(partial_gram, ("slab", "row", "col"))
    cells_total = (
        size_x
        * size_y
        * size_z
        * lax.axis_size("slab")
        * lax.axis_size("row")
        * lax.axis_size("col")
    )
    return (third, summed_gram / cells_total)


side = 32
lanes = 128
per_group = lanes // side
groups = side // per_group
margin = 32
low_groups = 2
low_rows = 16
box = 16
unroll = 8
centre = 0.5 * (upper_edge + lower_edge)
half_width = 0.5 * (upper_edge - lower_edge)
MESH = pl.DeviceIdType.MESH


def plane_matrices():
    span = 2 * per_group
    full = np.zeros((2 * span * side, 2 * span * side), np.float64)
    index = np.arange(2 * span * side)
    x, y = index // side, index % side
    dx = np.abs(x[:, None] - x[None])
    dy = np.abs(y[:, None] - y[None])
    for reach in range(1, 7):
        near = ((dx == reach) & (dy == 0)) | ((dx == 0) & (dy == reach))
        full[near] = -0.5 / half_width * stencil_weights[reach]
    cut = span * side
    parts = []
    for part in (full[:cut, :cut], full[:cut, cut:], full[cut:, :cut]):
        high = part.astype(ml_dtypes.bfloat16)
        parts += [high, (part - high.astype(np.float64)).astype(ml_dtypes.bfloat16)]
    return np.stack(parts)


def split_three(value):
    first = value.astype(jnp.bfloat16).astype(jnp.float32)
    second = (value - first).astype(jnp.bfloat16).astype(jnp.float32)
    return (first, second, value - first - second)


def build_tables(offsets, beta, tables):
    points = beta.shape[1]
    for kind in range(beta.shape[0]):
        dx = offsets[kind, 0:1, :] + 5
        dy = offsets[kind, 1:2, :] + 5
        dz = offsets[kind, 2:3, :] + 5
        parts = split_three(beta[kind : kind + 1, :])
        for phase in range(per_group):
            moved = dx + phase
            place = (moved // per_group) * box + dz
            lane = (moved % per_group) * side + dy
            hit = lax.broadcasted_iota(jnp.int32, (4 * box, points), 0) == place
            left = jnp.concatenate([jnp.where(hit, part, 0.0) for part in parts], axis=0)
            right = (lax.broadcasted_iota(jnp.int32, (lanes, points), 0) == lane).astype(jnp.float32)
            dense = lax.dot_general(
                left.astype(jnp.bfloat16),
                right.astype(jnp.bfloat16),
                (((1,), (1,)), ((), ())),
                preferred_element_type=jnp.float32,
            )
            tables[kind * per_group + phase] = (
                dense[: 4 * box] + dense[4 * box : 8 * box] + dense[8 * box :]
            )


def spread_kernel(
    shape, wave, potential, positions, species, counts, offsets, beta, field_out, potential_out, atoms_out, tables,
    got, info, local_sem, send_sem, recv_sem, part_send, part_recv, pair_send, pair_recv,
):
    slabs, rows, _ = shape
    depth = wave.shape[3]
    slab, row, col = (lax.axis_index(name) for name in ("slab", "row", "col"))
    me = slab * rows + row
    other = (slab, row, 1 - col)
    shifts = [(s, r) for s in (1, 2, 3, 0) for r in range(rows)]

    def partner(shift):
        return (lax.rem(slab + shift[0], slabs), lax.rem(row + shift[1], rows), col)

    barrier = pltpu.get_barrier_semaphore()
    for shift in shifts:
        if shift != (0, 0):
            pl.semaphore_signal(barrier, inc=1, device_id=partner(shift), device_id_type=MESH)
    pl.semaphore_signal(barrier, inc=1, device_id=other, device_id_type=MESH)

    slots = positions.shape[1]
    live = (lax.broadcasted_iota(jnp.int32, (1, slots), 1) < counts[0]).astype(jnp.int32)
    words = [positions[0:1, :], positions[1:2, :], positions[2:3, :], species[...].reshape(1, slots), live]
    words.append(jnp.zeros((1, lanes - 5 * slots), jnp.int32))
    info[...] = jnp.concatenate(words, axis=1)
    pl.semaphore_wait(barrier, slabs * rows)

    def remote(source, place, send, recv, device):
        copy = pltpu.make_async_remote_copy(
            src_ref=source,
            dst_ref=place,
            send_sem=send,
            recv_sem=recv,
            device_id=device,
            device_id_type=MESH,
        )
        copy.start()
        return copy

    def local(source, place, sem):
        copy = pltpu.make_async_copy(source, place, sem)
        copy.start()
        return copy

    first = [
        local(potential, got.at[1, me], local_sem.at[1]),
        local(info, atoms_out.at[col, me], local_sem.at[2]),
    ]
    for r in range(1, rows):
        device = partner((0, r))
        first.append(remote(potential, got.at[1, me], part_send.at[0, r], part_recv.at[0, r], device))
        first.append(remote(info, atoms_out.at[col, me], part_send.at[1, r], part_recv.at[1, r], device))
    moves = {}
    for index, shift in enumerate(shifts):
        if shift == (0, 0):
            moves[shift] = local(wave.at[me], got.at[0, me], local_sem.at[0])
        else:
            device = partner(shift)
            target = device[0] * rows + device[1]
            moves[shift] = remote(wave.at[target], got.at[0, me], send_sem.at[index], recv_sem.at[index], device)
    for copy in first:
        copy.wait()
    run = pl.ds(slab * rows, rows)
    second = []
    for s in range(1, slabs):
        device = partner((s, 0))
        second.append(remote(got.at[1, run], got.at[1, run], part_send.at[2, s], part_recv.at[2, s], device))
        second.append(
            remote(atoms_out.at[col, run], atoms_out.at[col, run], part_send.at[3, s], part_recv.at[3, s], device)
        )
    build_tables(offsets, beta, tables)
    for copy in second:
        copy.wait()

    own_at = pl.multiple_of(col * margin, margin)
    from_at = pl.multiple_of(col * margin + (1 - col) * (depth - margin), margin)
    to_at = pl.multiple_of(col * depth, margin)

    def turn(kind, out, part):
        for half in range(2):
            tiles = [
                got[kind, part * rows + r, half * per_group + x] for x in range(per_group) for r in range(rows)
            ]
            out[part * 2 + half, pl.ds(own_at, depth), :] = jnp.concatenate(tiles, axis=0).T

    def pass_on(out, part, size, index):
        source = out.at[pl.ds(part * 2, size), pl.ds(from_at, margin), :]
        place = out.at[pl.ds(part * 2, size), pl.ds(to_at, margin), :]
        return remote(source, place, pair_send.at[index], pair_recv.at[index], other)

    last = [remote(atoms_out.at[col], atoms_out.at[col], pair_send.at[0], pair_recv.at[0], other)]
    for part in range(slabs):
        turn(1, potential_out, part)
    last.append(pass_on(potential_out, 0, groups, 1))
    for order, s in enumerate((1, 2, 3, 0)):
        for r in range(rows):
            moves[(s, r)].wait()
        part = lax.rem(slab + (slabs - s), slabs)
        turn(0, field_out, part)
        last.append(pass_on(field_out, part, 2, 2 + order))
    for copy in last:
        copy.wait()


def filter_kernel(
    rows, atoms, coupling, field, potential, tables, matrices_in, out,
    ping, pong, plane, high, low, matrices, shapes, listed, found, weights, matrix_sem,
):
    window = field.shape[1]
    depth = out.shape[3]
    slots = 8
    col = lax.axis_index("col")
    window_start = col * (depth - margin)
    inner = pl.ds(low_rows, window)
    matrix_copy = pltpu.make_async_copy(matrices_in, matrices, matrix_sem)
    matrix_copy.start()

    def clear_rims(ref):
        ref[:low_groups] = jnp.zeros((low_groups,) + ref.shape[1:], jnp.float32)
        ref[low_groups + groups :] = jnp.zeros((low_groups,) + ref.shape[1:], jnp.float32)
        middle = pl.ds(low_groups, groups)
        ref[middle, :low_rows] = jnp.zeros((groups, low_rows, lanes), jnp.float32)
        ref[middle, low_rows + window :] = jnp.zeros((groups, low_rows, lanes), jnp.float32)

    clear_rims(ping)
    ping[pl.ds(low_groups, groups), inner] = field[...]

    lane_y = lax.broadcasted_iota(jnp.int32, (4 * box, lanes), 1) % side

    def find(block, count):
        for place in range(slots):
            local = atoms[block, 0, 2 * slots + place] - window_start
            live = atoms[block, 0, 4 * slots + place]
            listed[count] = block * slots + place
            count = count + jnp.where((local >= -5) & (local <= window + 4), live, 0)
        return count

    count = lax.fori_loop(0, atoms.shape[0], find, jnp.int32(0))
    for extra in range(unroll):
        listed[count + extra] = 0
    batches = (count + unroll - 1) // unroll

    def shape_batch(index, carry):
        for extra in range(unroll):
            atom = index * unroll + extra
            slot = listed[atom]
            block, place = slot // slots, lax.rem(slot, slots)
            x, y, z, kind = (atoms[block, 0, word * slots + place] for word in range(4))
            found[0, atom] = (x + 3) // per_group
            found[1, atom] = jnp.clip(z - window_start, -5, window + 4) - 5 + low_rows
            weights[atom] = jnp.where(atom < count, coupling[kind] / half_width, 0.0)
            start = y - 5
            table = tables[kind * per_group + lax.rem(x + 3, per_group)]
            rolled = pltpu.roll(table, lax.rem(start + lanes, lanes), 1)
            shapes[atom] = jnp.where((lane_y >= start) & (lane_y <= start + 10), rolled, 0.0)
        return carry

    lax.fori_loop(0, batches, shape_batch, 0)
    matrix_copy.wait()

    def step(source, target, scale, keep):
        for tile in range(groups // 2):
            wide = jnp.concatenate(
                [source[low_groups + 2 * tile, inner], source[low_groups + 2 * tile + 1, inner]], axis=1
            )
            big = wide.astype(jnp.bfloat16)
            high[pl.ds(tile * window, window)] = big
            low[pl.ds(tile * window, window)] = (wide - big.astype(jnp.float32)).astype(jnp.bfloat16)
        total = groups // 2 * window

        def product(part, which, begin, end):
            return jnp.dot(part[begin:end], matrices[which], preferred_element_type=jnp.float32)

        def triple(which, begin, end):
            return (
                product(high, which, begin, end)
                + product(low, which, begin, end)
                + product(high, which + 1, begin, end)
            )

        plane[...] = triple(0, 0, total)
        plane[window:] += triple(2, 0, total - window)
        plane[: total - window] += triple(4, window, total)

        for group in range(groups):
            padded = low_groups + group
            diagonal = (potential[group] - (centre + 1.5 * stencil_weights[0])) / half_width
            value = diagonal * source[padded, inner]
            for reach in range(1, 7):
                value = value + (-0.5 / half_width * stencil_weights[reach]) * (
                    source[padded, pl.ds(low_rows + reach, window)]
                    + source[padded, pl.ds(low_rows - reach, window)]
                )
            half = group % 2 * lanes
            value = value + plane[pl.ds(group // 2 * window, window), half : half + lanes]
            if keep:
                value = scale * value - target[padded, inner]
            target[padded, inner] = value

        def batch(index, carry):
            base = index * unroll
            gains = []
            for extra in range(unroll):
                atom = base + extra
                group, at = found[0, atom], found[1, atom]
                total = jnp.zeros((box, lanes), jnp.float32)
                for part in range(4):
                    total = total + source[group + part, pl.ds(at, box)] * shapes[atom, pl.ds(part * box, box)]
                summed = jnp.sum(jnp.sum(total, axis=0, keepdims=True), axis=1, keepdims=True)
                gains.append(summed * (weights[atom] * scale))
            for extra in range(unroll):
                atom = base + extra
                group, at = found[0, atom], found[1, atom]
                for part in range(4):
                    target[group + part, pl.ds(at, box)] += gains[extra] * shapes[atom, pl.ds(part * box, box)]
            return carry

        lax.fori_loop(0, batches, batch, 0)
        clear_rims(target)

    step(ping, pong, 1.0, False)
    step(pong, ping, 2.0, True)
    step(ping, pong, 2.0, True)

    begin = pl.multiple_of(low_rows + col * margin, 16)
    for group in range(groups):
        turned = pong[low_groups + group, pl.ds(begin, depth), :].T
        for x in range(per_group):
            for r in range(rows):
                at = (x * rows + r) * 8
                out[group // 2 * rows + r, group % 2 * per_group + x] = turned[at : at + 8]


def collect_kernel(
    shape, cells, pieces, block, gram, partial, sums, local_sem, send_sem, recv_sem, sum_send, sum_recv
):
    slabs, rows, cols = shape
    bands = pieces.shape[0]
    devices = slabs * rows * cols
    slab, row, col = (lax.axis_index(name) for name in ("slab", "row", "col"))
    me = slab * rows + row
    mine = me * cols + col

    def partner(step):
        target = lax.rem(mine + step, devices)
        return (target // (rows * cols), lax.rem(target // cols, rows), lax.rem(target, cols))

    barrier = pltpu.get_barrier_semaphore()
    for step in range(1, devices):
        pl.semaphore_signal(barrier, inc=1, device_id=partner(step), device_id_type=MESH)
    pl.semaphore_wait(barrier, devices - 1)

    copies = [pltpu.make_async_copy(pieces.at[me], block.at[me], local_sem)]
    for step in range(1, bands):
        target = lax.rem(me + step, bands)
        copies.append(
            pltpu.make_async_remote_copy(
                src_ref=pieces.at[target],
                dst_ref=block.at[me],
                send_sem=send_sem.at[step],
                recv_sem=recv_sem.at[step],
                device_id=(target // rows, lax.rem(target, rows), col),
                device_id_type=MESH,
            )
        )
    for copy in copies:
        copy.start()
    for copy in copies:
        copy.wait()

    size_x, size_y = block.shape[1:3]
    flat = bands * size_y
    wide = jnp.concatenate([block[:, x].reshape(flat, lanes) for x in range(size_x)], axis=1)
    high = wide.astype(jnp.bfloat16)
    low = (wide - high.astype(jnp.float32)).astype(jnp.bfloat16)
    product = lax.dot_general(
        high,
        jnp.concatenate([high, low], axis=0),
        (((1,), (1,)), ((), ())),
        preferred_element_type=jnp.float32,
    )
    cross = product[:, flat:]
    product = product[:, :flat] + cross + cross.T
    one = lax.broadcasted_iota(jnp.int32, (flat, flat), 0)
    two = lax.broadcasted_iota(jnp.int32, (flat, flat), 1)
    product = jnp.where(one % size_y == two % size_y, product, 0.0)
    product = jnp.sum(product.reshape(bands, size_y, flat), axis=1)

    def times(value, picks):
        parts = jnp.concatenate(split_three(value), axis=0).astype(jnp.bfloat16)
        result = jnp.dot(parts, picks.astype(jnp.bfloat16), preferred_element_type=jnp.float32)
        return result[:bands] + result[bands : 2 * bands] + result[2 * bands :]

    folded = times(product, (one // size_y == two % bands).astype(jnp.float32))
    packed = (2, bands // 2, lanes)
    keep = lax.broadcasted_iota(jnp.int32, packed, 1) == lax.broadcasted_iota(jnp.int32, packed, 2) // bands
    partial[...] = jnp.sum(jnp.where(keep, folded.reshape(packed), 0.0), axis=1)
    sums[mine] = partial[...]
    copies = []
    for step in range(1, devices):
        copies.append(
            pltpu.make_async_remote_copy(
                src_ref=partial,
                dst_ref=sums.at[mine],
                send_sem=sum_send.at[step],
                recv_sem=sum_recv.at[step],
                device_id=partner(step),
                device_id_type=MESH,
            )
        )
    for copy in copies:
        copy.start()
    for copy in copies:
        copy.wait()
    total = jnp.sum(sums[...], axis=0) * (1.0 / cells)
    total = jnp.where(keep, jnp.broadcast_to(total[:, None, :], packed), 0.0).reshape(bands, lanes)
    gram[...] = times(total, (one % bands == two).astype(jnp.float32))[:, :bands]


def band_shards(shape, wave, potential, positions, species, counts, offsets, beta, coupling):
    slabs, rows, cols = shape
    bands, size_x, size_y, size_z = wave.shape
    slots = positions.shape[1]
    window = size_z + margin
    vmem = pl.BlockSpec(memory_space=pltpu.VMEM)
    smem = pl.BlockSpec(memory_space=pltpu.SMEM)
    hbm = pl.BlockSpec(memory_space=pltpu.HBM)
    dma = pltpu.SemaphoreType.DMA
    table_count = beta.shape[0] * per_group
    field, wide_potential, atoms, tables = pl.pallas_call(
        lambda *refs: spread_kernel(shape, *refs),
        out_shape=(
            jax.ShapeDtypeStruct((groups, window, lanes), jnp.float32),
            jax.ShapeDtypeStruct((groups, window, lanes), jnp.float32),
            jax.ShapeDtypeStruct((cols, bands, 1, lanes), jnp.int32),
            jax.ShapeDtypeStruct((table_count, 4 * box, lanes), jnp.float32),
        ),
        in_specs=[hbm, hbm, vmem, vmem, smem, vmem, vmem],
        out_specs=[vmem] * 4,
        scratch_shapes=[
            pltpu.VMEM((2, bands, size_x, size_y, size_z), jnp.float32),
            pltpu.VMEM((1, lanes), jnp.int32),
            dma((3,)),
            dma((bands,)),
            dma((bands,)),
            dma((4, 4)),
            dma((4, 4)),
            dma((6,)),
            dma((6,)),
        ],
        compiler_params=pltpu.CompilerParams(
            collective_id=0, has_side_effects=True, vmem_limit_bytes=32 * 2**20
        ),
        name="spread",
    )(wave, potential, positions, species, counts, offsets, beta)

    most = bands * cols * slots + unroll
    pieces = pl.pallas_call(
        lambda *refs: filter_kernel(rows, *refs),
        out_shape=jax.ShapeDtypeStruct(wave.shape, jnp.float32),
        in_specs=[smem, smem, vmem, vmem, vmem, hbm],
        out_specs=vmem,
        scratch_shapes=[
            pltpu.VMEM((groups + 2 * low_groups, window + 2 * low_rows, lanes), jnp.float32),
            pltpu.VMEM((groups + 2 * low_groups, window + 2 * low_rows, lanes), jnp.float32),
            pltpu.VMEM((groups // 2 * window, 2 * lanes), jnp.float32),
            pltpu.VMEM((groups // 2 * window, 2 * lanes), jnp.bfloat16),
            pltpu.VMEM((groups // 2 * window, 2 * lanes), jnp.bfloat16),
            pltpu.VMEM((6, 2 * lanes, 2 * lanes), jnp.bfloat16),
            pltpu.VMEM((most, 4 * box, lanes), jnp.float32),
            pltpu.SMEM((most,), jnp.int32),
            pltpu.SMEM((2, most), jnp.int32),
            pltpu.SMEM((most,), jnp.float32),
            dma,
        ],
        compiler_params=pltpu.CompilerParams(vmem_limit_bytes=40 * 2**20),
        name="chebyshev",
    )(
        atoms.reshape(cols * bands, 1, lanes),
        coupling,
        field,
        wide_potential,
        tables,
        jnp.asarray(plane_matrices()),
    )

    devices = slabs * rows * cols
    cells = devices * size_x * size_y * size_z
    filtered, gram = pl.pallas_call(
        lambda *refs: collect_kernel(shape, cells, *refs),
        out_shape=(
            jax.ShapeDtypeStruct(wave.shape, jnp.float32),
            jax.ShapeDtypeStruct((bands, bands), jnp.float32),
        ),
        in_specs=[vmem],
        out_specs=[vmem] * 2,
        scratch_shapes=[
            pltpu.VMEM((2, lanes), jnp.float32),
            pltpu.VMEM((devices, 2, lanes), jnp.float32),
            dma,
            dma((bands,)),
            dma((bands,)),
            dma((devices,)),
            dma((devices,)),
        ],
        compiler_params=pltpu.CompilerParams(
            collective_id=1, has_side_effects=True, vmem_limit_bytes=32 * 2**20
        ),
        name="collect",
    )(pieces)
    return filtered, gram


def solution(mesh):
    in_specs = (
        P(None, "slab", "row", "col"),
        P("slab", "row", "col"),
        P(None, ("slab", "row", "col")),
        P(("slab", "row", "col")),
        P(("slab", "row", "col")),
        P(),
        P(),
        P(),
    )
    out_specs = (P(None, "slab", "row", "col"), P())
    shape = tuple(mesh.shape[name] for name in ("slab", "row", "col"))

    def run(*arrays):
        bands, size_x, size_y, size_z = arrays[0].shape
        one_band_a_chip = (
            shape[0] * shape[1] == bands
            and shape[2] == 2
            and (size_x, size_y, size_z) == (shape[0] * 8, shape[1] * 8, 2 * lanes)
            and (size_x, size_y) == (side, side)
            and arrays[2].shape[1] == 8 * mesh.size
        )
        body = (lambda *blocks: band_shards(shape, *blocks)) if one_band_a_chip else shards
        return jax.shard_map(
            body, mesh=mesh, in_specs=in_specs, out_specs=out_specs, check_vma=False
        )(*arrays)

    return run
```

profile of v0, /device:TPU:0, one launch (start us, length us, event | category | flops | bytes accessed | tf_op | source)
XLA Modules:
  0.0 69.5 jit_solution(16434015346460166495)
XLA Ops:
  0.6 0.0 copy-start.2
  1.3 0.0 copy-start.3
  1.3 0.0 copy-start.4
  1.3 0.0 copy-start.5
  1.3 0.7 %copy.11.refs_5_ = s32[4,3,384]{2,1,0:T(4,128)S(1)} copy(s32[4,3,384]{2,0,1:T(4,128)} %param.14) | data formatting | bytes 36864 | tf_op args[5]
  2.1 0.0 copy-done.2
  2.1 0.0 copy-done.3
  2.1 0.0 copy-done.4
  2.1 0.0 copy-done.5
  2.1 0.0 copy-start.1
  2.1 1.0 %copy-done.1 = f32[16,8,8,128]{3,2,1,0:T(8,128)S(1)} copy-done((f32[16,8,8,128]{3,2,1,0:T(8,128)S(1)}, f32[16,8,8,128]{3,2,1,0:T(8,128)}, u32[]{:S(2)}) %copy-start.1) | copy-done | bytes 524312
  3.2 23.3 %spread.1 = (f32[8,160,128]{2,1,0:T(8,128)S(1)}, f32[8,160,128]{2,1,0:T(8,128)S(1)}, s32[2,16,1,128]{3,2,1,0:T(1,128)S(1)}, f32[16,64,128]{2,1,0:T(8,128)S(1)}) custom-call(f32[16,8,8,128]{3,2,1,0:T(8,128)S(1)} %copy-done.1, f32[8,8,128]{2,1,0:T(8,128)S(1)} %copy-done.2, s32[3,8]{1,0:T(4,128)S(1)} %copy-done.4, s32[8]{0:T(128)S(1)} %copy-done.5, ...), custom_call_target="tpu_custom_call" | custom-call | tf_op jit(solution)/shard_map/spread/pallas_call | solution.py:541
  26.5 0.0 copy-start.6
  26.5 0.6 copy-done.6
  27.1 0.0 copy-start
  27.1 1.1 %copy-done = bf16[6,256,256]{2,1,0:T(8,128)(2,1)S(1)} copy-done((bf16[6,256,256]{2,1,0:T(8,128)(2,1)S(1)}, bf16[6,256,256]{2,1,0:T(8,128)(2,1)}, u32[]{:S(2)}) %copy-start) | copy-done | bytes 786456
  28.3 14.3 %chebyshev.1.refs_0_ = f32[16,8,8,128]{3,2,1,0:T(8,128)S(1)} custom-call(s32[32,1,128]{2,1,0:T(1,128)S(1)} %bitcast.1, f32[4]{0:T(128)S(1)} %copy-done.6, f32[8,160,128]{2,1,0:T(8,128)S(1)} %get-tuple-element.7.refs_2_, f32[8,160,128]{2,1,0:T(8,128)S(1)} %get-tuple-element.8.refs_3_, f32[16,64,128]{2,1,0:T(8,128)S(1)} %get-tuple-element.9.refs_4_, ...), custom_call_target="tpu_custom_call" | custom-call | tf_op jit(solution)/shard_map/chebyshev/pallas_call | solution.py:569
  42.6 25.5 %collect.1 = (f32[16,8,8,128]{3,2,1,0:T(8,128)S(1)}, f32[16,16]{1,0:T(8,128)S(1)}) custom-call(f32[16,8,8,128]{3,2,1,0:T(8,128)S(1)} %chebyshev.1.refs_0_), custom_call_target="tpu_custom_call" | custom-call | tf_op jit(solution)/shard_map/collect/pallas_call | solution.py:600
  68.1 0.8 %copy.15 = f32[16,8,8,128]{3,2,1,0:T(8,128)} copy(f32[16,8,8,128]{3,2,1,0:T(8,128)S(1)} %get-tuple-element.12) | data formatting | bytes 1048576
  68.9 0.6 copy.16
Async XLA Ops:
  0.6 1.4 %copy-start.2 = (f32[8,8,128]{2,1,0:T(8,128)S(1)}, f32[8,8,128]{2,1,0:T(8,128)}, u32[]{:S(2)}) copy-start(f32[8,8,128]{2,1,0:T(8,128)} %refs_1_.2) | copy-start | bytes 98308
  1.3 0.8 %copy-start.3 = (f32[4,384]{1,0:T(4,128)S(1)}, f32[4,384]{1,0:T(4,128)}, u32[]{:S(2)}) copy-start(f32[4,384]{1,0:T(4,128)} %refs_6_.1) | copy-start | bytes 18436
  1.3 0.8 %copy-start.4 = (s32[3,8]{1,0:T(4,128)S(1)}, s32[3,8]{1,0:T(4,128)}, u32[]{:S(2)}) copy-start(s32[3,8]{1,0:T(4,128)} %refs_2_.1) | copy-start | bytes 292
  1.3 0.8 %copy-start.5 = (s32[8]{0:T(128)S(1)}, s32[8]{0:T(128)}, u32[]{:S(2)}) copy-start(s32[8]{0:T(128)} %refs_3_.1) | copy-start | bytes 100
  2.1 1.0 %copy-start.1 = (f32[16,8,8,128]{3,2,1,0:T(8,128)S(1)}, f32[16,8,8,128]{3,2,1,0:T(8,128)}, u32[]{:S(2)}) copy-start(f32[16,8,8,128]{3,2,1,0:T(8,128)} %refs_0_.1) | copy-start | bytes 1572868
  26.5 0.7 copy-start.6
  27.1 1.1 %copy-start = (bf16[6,256,256]{2,1,0:T(8,128)(2,1)S(1)}, bf16[6,256,256]{2,1,0:T(8,128)(2,1)}, u32[]{:S(2)}) copy-start(bf16[6,256,256]{2,1,0:T(8,128)(2,1)} %constant.2.clone.refs_5_) | copy-start | bytes 2359300
where the time goes:
time: 69.9 us; the launch traced here: 69.5 us
  Pallas kernels  63.1 us (90%)
  local copies, waits for them, and re-layouts  4.98 us (7%)
  between operations  1.39 us (2%)
    pallas_call x1, Pallas kernels, band_shards(): pl.pallas_call(lambda *refs: collect_kernel(shape, cells, *refs), out_sha...  25.5 us
    pallas_call x1, Pallas kernels, band_shards(): pl.pallas_call(lambda *refs: spread_kernel(shape, *refs), out_shape=(jax....  23.3 us
    pallas_call x1, Pallas kernels, band_shards(): pl.pallas_call(lambda *refs: filter_kernel(rows, *refs), out_shape=jax.Sh...  14.3 us
    unnamed x17, local copies, waits for them, and re-layouts  4.98 us

commit v1 on v0

--- a/solution.py
+++ b/solution.py
@@ -160,22 +160,24 @@
 MESH = pl.DeviceIdType.MESH
 
 
-def plane_matrices():
+def build_matrices(matrices):
     span = 2 * per_group
-    full = np.zeros((2 * span * side, 2 * span * side), np.float64)
-    index = np.arange(2 * span * side)
-    x, y = index // side, index % side
-    dx = np.abs(x[:, None] - x[None])
-    dy = np.abs(y[:, None] - y[None])
-    for reach in range(1, 7):
-        near = ((dx == reach) & (dy == 0)) | ((dx == 0) & (dy == reach))
-        full[near] = -0.5 / half_width * stencil_weights[reach]
-    cut = span * side
-    parts = []
-    for part in (full[:cut, :cut], full[:cut, cut:], full[cut:, :cut]):
-        high = part.astype(ml_dtypes.bfloat16)
-        parts += [high, (part - high.astype(np.float64)).astype(ml_dtypes.bfloat16)]
-    return np.stack(parts)
+    size = span * side
+    one = lax.broadcasted_iota(jnp.int32, (size, size), 0)
+    two = lax.broadcasted_iota(jnp.int32, (size, size), 1)
+    dy = jnp.abs(one % side - two % side)
+    for which, shift in enumerate((0, span, -span)):
+        dx = jnp.abs(one // side - two // side - shift)
+        distance = jnp.where(dy == 0, dx, jnp.where(dx == 0, dy, 0))
+        high = jnp.zeros((size, size), jnp.float32)
+        low = jnp.zeros((size, size), jnp.float32)
+        for reach in range(1, 7):
+            weight = -0.5 / half_width * stencil_weights[reach]
+            top = float(np.float32(ml_dtypes.bfloat16(weight)))
+            high = jnp.where(distance == reach, top, high)
+            low = jnp.where(distance == reach, weight - top, low)
+        matrices[2 * which] = high.astype(jnp.bfloat16)
+        matrices[2 * which + 1] = low.astype(jnp.bfloat16)
 
 
 def split_three(value):
@@ -187,9 +189,7 @@
 def build_tables(offsets, beta, tables):
     points = beta.shape[1]
     for kind in range(beta.shape[0]):
-        dx = offsets[kind, 0:1, :] + 5
-        dy = offsets[kind, 1:2, :] + 5
-        dz = offsets[kind, 2:3, :] + 5
+        dx, dy, dz = (offsets[axis, kind : kind + 1, :] + 5 for axis in range(3))
         parts = split_three(beta[kind : kind + 1, :])
         for phase in range(per_group):
             moved = dx + phase
@@ -210,8 +210,8 @@
 
 
 def spread_kernel(
-    shape, wave, potential, positions, species, counts, offsets, beta, field_out, potential_out, atoms_out, tables,
-    got, info, local_sem, send_sem, recv_sem, part_send, part_recv, pair_send, pair_recv,
+    shape, wave, potential, positions, species, counts, offsets, beta, coupling,
+    field_out, potential_out, atoms_out, tables, matrices, strengths, got, info, local_sem, send_sem, recv_sem, part_send, part_recv, pair_send, pair_recv,
 ):
     slabs, rows, _ = shape
     depth = wave.shape[3]
@@ -280,6 +280,11 @@
             remote(atoms_out.at[col, run], atoms_out.at[col, run], part_send.at[3, s], part_recv.at[3, s], device)
         )
     build_tables(offsets, beta, tables)
+    build_matrices(matrices)
+    kinds = beta.shape[0]
+    for kind in range(kinds):
+        strengths[kind] = jnp.full((1, lanes), 1.0 / half_width, jnp.float32) * coupling[kind]
+    strengths[kinds] = jnp.zeros((1, lanes), jnp.float32)
     for copy in second:
         copy.wait()
 
@@ -313,18 +318,56 @@
         copy.wait()
 
 
+def plane_part(source, matrices, plane, high, low, window):
+    inner = pl.ds(low_rows, window)
+    for tile in range(groups // 2):
+        wide = jnp.concatenate(
+            [source[low_groups + 2 * tile, inner], source[low_groups + 2 * tile + 1, inner]], axis=1
+        )
+        big = wide.astype(jnp.bfloat16)
+        high[pl.ds(tile * window, window)] = big
+        low[pl.ds(tile * window, window)] = (wide - big.astype(jnp.float32)).astype(jnp.bfloat16)
+    total = groups // 2 * window
+
+    def product(part, which, begin, end):
+        return jnp.dot(part[begin:end], matrices[which], preferred_element_type=jnp.float32)
+
+    def triple(which, begin, end):
+        return (
+            product(high, which, begin, end)
+            + product(low, which, begin, end)
+            + product(high, which + 1, begin, end)
+        )
+
+    plane[...] = triple(0, 0, total)
+    plane[window:] += triple(2, 0, total - window)
+    plane[: total - window] += triple(4, window, total)
+
+
+def local_part(source, potential, plane, part, half, window):
+    group = 2 * part + half
+    padded = low_groups + group
+    diagonal = (potential[group] - (centre + 1.5 * stencil_weights[0])) / half_width
+    value = diagonal * source[padded, pl.ds(low_rows, window)]
+    for reach in range(1, 7):
+        value = value + (-0.5 / half_width * stencil_weights[reach]) * (
+            source[padded, pl.ds(low_rows + reach, window)] + source[padded, pl.ds(low_rows - reach, window)]
+        )
+    at = part * window
+    if not isinstance(part, int):
+        at = pl.multiple_of(at, 32)
+    return value + plane[pl.ds(at, window), half * lanes : (half + 1) * lanes]
+
+
 def filter_kernel(
-    rows, atoms, coupling, field, potential, tables, matrices_in, out,
-    ping, pong, plane, high, low, matrices, shapes, listed, found, weights, matrix_sem,
+    depth, atoms, field, potential, tables, matrices, strengths, ping, pong,
+    plane, high, low, shapes, listed, found,
 ):
     window = field.shape[1]
-    depth = out.shape[3]
     slots = 8
     col = lax.axis_index("col")
     window_start = col * (depth - margin)
     inner = pl.ds(low_rows, window)
-    matrix_copy = pltpu.make_async_copy(matrices_in, matrices, matrix_sem)
-    matrix_copy.start()
 
     def clear_rims(ref):
         ref[:low_groups] = jnp.zeros((low_groups,) + ref.shape[1:], jnp.float32)
@@ -349,7 +392,7 @@
     count = lax.fori_loop(0, atoms.shape[0], find, jnp.int32(0))
     for extra in range(unroll):
         listed[count + extra] = 0
-    batches = (count + unroll - 1) // unroll
+    batches = jnp.maximum((count + unroll - 1) // unroll, 1)
 
     def shape_batch(index, carry):
         for extra in range(unroll):
@@ -359,7 +402,7 @@
             x, y, z, kind = (atoms[block, 0, word * slots + place] for word in range(4))
             found[0, atom] = (x + 3) // per_group
             found[1, atom] = jnp.clip(z - window_start, -5, window + 4) - 5 + low_rows
-            weights[atom] = jnp.where(atom < count, coupling[kind] / half_width, 0.0)
+            found[2, atom] = jnp.where(atom < count, kind, strengths.shape[0] - 1)
             start = y - 5
             table = tables[kind * per_group + lax.rem(x + 3, per_group)]
             rolled = pltpu.roll(table, lax.rem(start + lanes, lanes), 1)
@@ -367,86 +410,61 @@
         return carry
 
     lax.fori_loop(0, batches, shape_batch, 0)
-    matrix_copy.wait()
+
+    def gather(source, index, scale):
+        gains = []
+        for extra in range(unroll):
+            atom = index * unroll + extra
+            group, at = found[0, atom], found[1, atom]
+            total = jnp.zeros((box, lanes), jnp.float32)
+            for part in range(4):
+                total = total + source[group + part, pl.ds(at, box)] * shapes[atom, pl.ds(part * box, box)]
+            summed = jnp.sum(jnp.sum(total, axis=0, keepdims=True), axis=1, keepdims=True)
+            gains.append(summed * (strengths[found[2, atom]] * scale))
+        return tuple(gains)
+
+    def scatter(target, index, gains):
+        for extra in range(unroll):
+            atom = index * unroll + extra
+            group, at = found[0, atom], found[1, atom]
+            for part in range(4):
+                target[group + part, pl.ds(at, box)] += gains[extra] * shapes[atom, pl.ds(part * box, box)]
+
+    def project(source, target, scale):
+        def batch(index, gains):
+            later = gather(source, index, scale)
+            scatter(target, index - 1, gains)
+            return later
+
+        gains = lax.fori_loop(1, batches, batch, gather(source, 0, scale))
+        scatter(target, batches - 1, gains)
 
     def step(source, target, scale, keep):
-        for tile in range(groups // 2):
-            wide = jnp.concatenate(
-                [source[low_groups + 2 * tile, inner], source[low_groups + 2 * tile + 1, inner]], axis=1
-            )
-            big = wide.astype(jnp.bfloat16)
-            high[pl.ds(tile * window, window)] = big
-            low[pl.ds(tile * window, window)] = (wide - big.astype(jnp.float32)).astype(jnp.bfloat16)
-        total = groups // 2 * window
-
-        def product(part, which, begin, end):
-            return jnp.dot(part[begin:end], matrices[which], preferred_element_type=jnp.float32)
-
-        def triple(which, begin, end):
-            return (
-                product(high, which, begin, end)
-                + product(low, which, begin, end)
-                + product(high, which + 1, begin, end)
-            )
-
-        plane[...] = triple(0, 0, total)
-        plane[window:] += triple(2, 0, total - window)
-        plane[: total - window] += triple(4, window, total)
-
-        for group in range(groups):
-            padded = low_groups + group
-            diagonal = (potential[group] - (centre + 1.5 * stencil_weights[0])) / half_width
-            value = diagonal * source[padded, inner]
-            for reach in range(1, 7):
-                value = value + (-0.5 / half_width * stencil_weights[reach]) * (
-                    source[padded, pl.ds(low_rows + reach, window)]
-                    + source[padded, pl.ds(low_rows - reach, window)]
-                )
-            half = group % 2 * lanes
-            value = value + plane[pl.ds(group // 2 * window, window), half : half + lanes]
-            if keep:
-                value = scale * value - target[padded, inner]
-            target[padded, inner] = value
-
-        def batch(index, carry):
-            base = index * unroll
-            gains = []
-            for extra in range(unroll):
-                atom = base + extra
-                group, at = found[0, atom], found[1, atom]
-                total = jnp.zeros((box, lanes), jnp.float32)
-                for part in range(4):
-                    total = total + source[group + part, pl.ds(at, box)] * shapes[atom, pl.ds(part * box, box)]
-                summed = jnp.sum(jnp.sum(total, axis=0, keepdims=True), axis=1, keepdims=True)
-                gains.append(summed * (weights[atom] * scale))
-            for extra in range(unroll):
-                atom = base + extra
-                group, at = found[0, atom], found[1, atom]
-                for part in range(4):
-                    target[group + part, pl.ds(at, box)] += gains[extra] * shapes[atom, pl.ds(part * box, box)]
-            return carry
-
-        lax.fori_loop(0, batches, batch, 0)
+        plane_part(source, matrices, plane, high, low, window)
+        for part in range(groups // 2):
+            for half in range(2):
+                padded = low_groups + 2 * part + half
+                value = local_part(source, potential, plane, part, half, window)
+                if keep:
+                    value = scale * value - target[padded, inner]
+                target[padded, inner] = value
+        project(source, target, scale)
         clear_rims(target)
 
     step(ping, pong, 1.0, False)
     step(pong, ping, 2.0, True)
-    step(ping, pong, 2.0, True)
-
-    begin = pl.multiple_of(low_rows + col * margin, 16)
-    for group in range(groups):
-        turned = pong[low_groups + group, pl.ds(begin, depth), :].T
-        for x in range(per_group):
-            for r in range(rows):
-                at = (x * rows + r) * 8
-                out[group // 2 * rows + r, group % 2 * per_group + x] = turned[at : at + 8]
+    middle = pl.ds(low_groups, groups)
+    pong[middle, inner] = -pong[middle, inner]
+    project(ping, pong, 2.0)
 
 
 def collect_kernel(
-    shape, cells, pieces, block, gram, partial, sums, local_sem, send_sem, recv_sem, sum_send, sum_recv
+    shape, cells, source, rest, potential, matrices, block, gram,
+    plane, high, low, turning, pieces, partial, sums, local_sem, send_sem, recv_sem, sum_send, sum_recv,
 ):
     slabs, rows, cols = shape
-    bands = pieces.shape[0]
+    bands, _, _, depth = block.shape
+    window = potential.shape[1]
     devices = slabs * rows * cols
     slab, row, col = (lax.axis_index(name) for name in ("slab", "row", "col"))
     me = slab * rows + row
@@ -459,23 +477,39 @@
     barrier = pltpu.get_barrier_semaphore()
     for step in range(1, devices):
         pl.semaphore_signal(barrier, inc=1, device_id=partner(step), device_id_type=MESH)
-    pl.semaphore_wait(barrier, devices - 1)
-
-    copies = [pltpu.make_async_copy(pieces.at[me], block.at[me], local_sem)]
-    for step in range(1, bands):
-        target = lax.rem(me + step, bands)
-        copies.append(
-            pltpu.make_async_remote_copy(
-                src_ref=pieces.at[target],
-                dst_ref=block.at[me],
-                send_sem=send_sem.at[step],
-                recv_sem=recv_sem.at[step],
-                device_id=(target // rows, lax.rem(target, rows), col),
-                device_id_type=MESH,
-            )
-        )
-    for copy in copies:
-        copy.start()
+    plane_part(source, matrices, plane, high, low, window)
+    begin = pl.multiple_of(col * margin, margin)
+    copies = []
+    for order, s in enumerate((1, 2, 3, 0)):
+        part = lax.rem(slab + s, slabs)
+        for half in range(2):
+            padded = low_groups + 2 * part + half
+            value = local_part(source, potential, plane, part, half, window)
+            turning[half] = 2.0 * value + rest[padded, pl.ds(low_rows, window)]
+            turned = turning[half, pl.ds(begin, depth), :].T
+            for x in range(per_group):
+                for r in range(rows):
+                    at = (x * rows + r) * 8
+                    pieces[part * rows + r, half * per_group + x] = turned[at : at + 8]
+        if order == 0:
+            pl.semaphore_wait(barrier, devices - 1)
+        for r in range(rows):
+            to_row = lax.rem(row + r, rows)
+            target = part * rows + to_row
+            if s == 0 and r == 0:
+                copies.append(pltpu.make_async_copy(pieces.at[me], block.at[me], local_sem))
+            else:
+                copies.append(
+                    pltpu.make_async_remote_copy(
+                        src_ref=pieces.at[target],
+                        dst_ref=block.at[me],
+                        send_sem=send_sem.at[order * rows + r],
+                        recv_sem=recv_sem.at[order * rows + r],
+                        device_id=(part, to_row, col),
+                        device_id_type=MESH,
+                    )
+                )
+            copies[-1].start()
     for copy in copies:
         copy.wait()
 
@@ -538,16 +572,19 @@
     hbm = pl.BlockSpec(memory_space=pltpu.HBM)
     dma = pltpu.SemaphoreType.DMA
     table_count = beta.shape[0] * per_group
-    field, wide_potential, atoms, tables = pl.pallas_call(
+    matrices_shape = jax.ShapeDtypeStruct((6, 2 * lanes, 2 * lanes), jnp.bfloat16)
+    field, wide_potential, atoms, tables, matrices, strengths = pl.pallas_call(
         lambda *refs: spread_kernel(shape, *refs),
         out_shape=(
             jax.ShapeDtypeStruct((groups, window, lanes), jnp.float32),
             jax.ShapeDtypeStruct((groups, window, lanes), jnp.float32),
             jax.ShapeDtypeStruct((cols, bands, 1, lanes), jnp.int32),
             jax.ShapeDtypeStruct((table_count, 4 * box, lanes), jnp.float32),
+            matrices_shape,
+            jax.ShapeDtypeStruct((beta.shape[0] + 1, 1, lanes), jnp.float32),
         ),
-        in_specs=[hbm, hbm, vmem, vmem, smem, vmem, vmem],
-        out_specs=[vmem] * 4,
+        in_specs=[hbm, hbm, vmem, vmem, smem, vmem, vmem, smem],
+        out_specs=[vmem] * 6,
         scratch_shapes=[
             pltpu.VMEM((2, bands, size_x, size_y, size_z), jnp.float32),
             pltpu.VMEM((1, lanes), jnp.int32),
@@ -563,37 +600,29 @@
             collective_id=0, has_side_effects=True, vmem_limit_bytes=32 * 2**20
         ),
         name="spread",
-    )(wave, potential, positions, species, counts, offsets, beta)
+    )(wave, potential, positions, species, counts, offsets.transpose(1, 0, 2), beta, coupling)
 
     most = bands * cols * slots + unroll
-    pieces = pl.pallas_call(
-        lambda *refs: filter_kernel(rows, *refs),
-        out_shape=jax.ShapeDtypeStruct(wave.shape, jnp.float32),
-        in_specs=[smem, smem, vmem, vmem, vmem, hbm],
-        out_specs=vmem,
-        scratch_shapes=[
-            pltpu.VMEM((groups + 2 * low_groups, window + 2 * low_rows, lanes), jnp.float32),
-            pltpu.VMEM((groups + 2 * low_groups, window + 2 * low_rows, lanes), jnp.float32),
-            pltpu.VMEM((groups // 2 * window, 2 * lanes), jnp.float32),
-            pltpu.VMEM((groups // 2 * window, 2 * lanes), jnp.bfloat16),
-            pltpu.VMEM((groups // 2 * window, 2 * lanes), jnp.bfloat16),
-            pltpu.VMEM((6, 2 * lanes, 2 * lanes), jnp.bfloat16),
+    padded = jax.ShapeDtypeStruct((groups + 2 * low_groups, window + 2 * low_rows, lanes), jnp.float32)
+    plane_scratch = [
+        pltpu.VMEM((groups // 2 * window, 2 * lanes), jnp.float32),
+        pltpu.VMEM((groups // 2 * window, 2 * lanes), jnp.bfloat16),
+        pltpu.VMEM((groups // 2 * window, 2 * lanes), jnp.bfloat16),
+    ]
+    second, rest = pl.pallas_call(
+        lambda *refs: filter_kernel(size_z, *refs),
+        out_shape=(padded, padded),
+        in_specs=[smem] + [vmem] * 5,
+        out_specs=[vmem] * 2,
+        scratch_shapes=plane_scratch
+        + [
             pltpu.VMEM((most, 4 * box, lanes), jnp.float32),
             pltpu.SMEM((most,), jnp.int32),
-            pltpu.SMEM((2, most), jnp.int32),
-            pltpu.SMEM((most,), jnp.float32),
-            dma,
+            pltpu.SMEM((3, most), jnp.int32),
         ],
         compiler_params=pltpu.CompilerParams(vmem_limit_bytes=40 * 2**20),
         name="chebyshev",
-    )(
-        atoms.reshape(cols * bands, 1, lanes),
-        coupling,
-        field,
-        wide_potential,
-        tables,
-        jnp.asarray(plane_matrices()),
-    )
+    )(atoms.reshape(cols * bands, 1, lanes), field, wide_potential, tables, matrices, strengths)
 
     devices = slabs * rows * cols
     cells = devices * size_x * size_y * size_z
@@ -603,9 +632,12 @@
             jax.ShapeDtypeStruct(wave.shape, jnp.float32),
             jax.ShapeDtypeStruct((bands, bands), jnp.float32),
         ),
-        in_specs=[vmem],
+        in_specs=[vmem] * 4,
         out_specs=[vmem] * 2,
-        scratch_shapes=[
+        scratch_shapes=plane_scratch
+        + [
+            pltpu.VMEM((2, window, lanes), jnp.float32),
+            pltpu.VMEM(wave.shape, jnp.float32),
             pltpu.VMEM((2, lanes), jnp.float32),
             pltpu.VMEM((devices, 2, lanes), jnp.float32),
             dma,
@@ -618,7 +650,7 @@
             collective_id=1, has_side_effects=True, vmem_limit_bytes=32 * 2**20
         ),
         name="collect",
-    )(pieces)
+    )(second, rest, wide_potential, matrices)
     return filtered, gram
 
 

time: 69.9 us -> 70.4 us (level)
  local copies, waits for them, and re-layouts: 4.98 us -> 6.59 us
  Pallas kernels: 63.1 us -> 62.1 us
    pallas_call x1, Pallas kernels: 25.5 us -> 23.5 us  [band_shards(): pl.pallas_call(lambda *refs: collect_kernel(shape, cells, *refs), out_sha...]
    unnamed x17 -> x16, local copies, waits for them, and re-layouts: 4.98 us -> 6.59 us
where the time goes in v1:
time: 70.4 us; the launch traced here: 70 us
  Pallas kernels  62.1 us (88%)
  local copies, waits for them, and re-layouts  6.59 us (9%)
  between operations  1.31 us (2%)
    pallas_call x1, Pallas kernels, band_shards(): pl.pallas_call(lambda *refs: spread_kernel(shape, *refs), out_shape=(jax....  23.9 us
    pallas_call x1, Pallas kernels, band_shards(): pl.pallas_call(lambda *refs: collect_kernel(shape, cells, *refs), out_sha...  23.5 us
    pallas_call x1, Pallas kernels, band_shards(): pl.pallas_call(lambda *refs: filter_kernel(size_z, *refs), out_shape=(pad...  14.8 us
    unnamed x16, local copies, waits for them, and re-layouts  6.59 us

profile of v1, /device:TPU:0, one launch (start us, length us, event | category | flops | bytes accessed | tf_op | source)
XLA Modules:
  0.0 70.0 jit_solution(16393332032880078098)
XLA Ops:
  1.3 0.0 copy-start
  1.3 1.0 %copy-done = f32[16,8,8,128]{3,2,1,0:T(8,128)S(1)} copy-done((f32[16,8,8,128]{3,2,1,0:T(8,128)S(1)}, f32[16,8,8,128]{3,2,1,0:T(8,128)}, u32[]{:S(2)}) %copy-start) | copy-done | bytes 524312
  2.3 0.0 copy-start.1
  2.3 0.8 %copy-done.1 = f32[8,8,128]{2,1,0:T(8,128)S(1)} copy-done((f32[8,8,128]{2,1,0:T(8,128)S(1)}, f32[8,8,128]{2,1,0:T(8,128)}, u32[]{:S(2)}) %copy-start.1) | copy-done | bytes 32792
  3.1 0.0 copy-start.2
  3.1 0.7 %copy-done.2 = s32[4,3,384]{2,0,1:T(4,128)S(1)} copy-done((s32[4,3,384]{2,0,1:T(4,128)S(1)}, s32[4,3,384]{2,0,1:T(4,128)}, u32[]{:S(2)}) %copy-start.2) | copy-done | bytes 18456
  3.8 0.0 copy-start.3
  3.8 0.7 copy-done.3
  4.5 0.0 copy-start.4
  4.5 0.7 copy-done.4
  5.2 0.0 copy-start.5
  5.2 0.7 copy-done.5
  5.8 0.0 copy-start.6
  5.8 0.7 copy-done.6
  6.5 23.9 %spread.1 = (f32[8,160,128]{2,1,0:T(8,128)S(1)}, f32[8,160,128]{2,1,0:T(8,128)S(1)}, s32[2,16,1,128]{3,2,1,0:T(1,128)S(1)}, f32[16,64,128]{2,1,0:T(8,128)S(1)}, ...) custom-call(f32[16,8,8,128]{3,2,1,0:T(8,128)S(1)} %copy-done, f32[8,8,128]{2,1,0:T(8,128)S(1)} %copy-done.1, ...), custom_call_target="tpu_custom_call" | custom-call | tf_op jit(solution)/shard_map/spread/pallas_call | solution.py:576
  30.4 14.8 %chebyshev.1 = (f32[12,192,128]{2,1,0:T(8,128)S(1)}, f32[12,192,128]{2,1,0:T(8,128)S(1)}) custom-call(s32[32,1,128]{2,1,0:T(1,128)S(1)} %bitcast.3, f32[8,160,128]{2,1,0:T(8,128)S(1)} %get-tuple-element.11.refs_1_, f32[8,160,128]{2,1,0:T(8,128)S(1)} %get-tuple-element.12.refs_2_, f32[16,64,128]{2,1,0:T(8,128)S(1)} %get-tuple-element.13.refs_3_, ...), custom_call_target="tpu_custom_call" | custom-call | tf_op jit(solution)/shard_map/chebyshev/pallas_call | solution.py:612
  45.1 23.5 %collect.1 = (f32[16,8,8,128]{3,2,1,0:T(8,128)S(1)}, f32[16,16]{1,0:T(8,128)S(1)}) custom-call(f32[12,192,128]{2,1,0:T(8,128)S(1)} %get-tuple-element.16.refs_0_, f32[12,192,128]{2,1,0:T(8,128)S(1)} %get-tuple-element.17.refs_1_, f32[8,160,128]{2,1,0:T(8,128)S(1)} %get-tuple-element.12.refs_2_, bf16[6,256,256]{2,1,0:T(8,128)(2,1)S(1)} %get-tuple-element.14.refs_4_.refs_3_), custom_call_target="tpu_custom_call" | custom-call | tf_op jit(solution)/shard_map/collect/pallas_call | solution.py:629
  68.6 0.8 %copy.13 = f32[16,8,8,128]{3,2,1,0:T(8,128)} copy(f32[16,8,8,128]{3,2,1,0:T(8,128)S(1)} %get-tuple-element.20) | data formatting | bytes 1048576
  69.4 0.6 copy.14
Async XLA Ops:
  1.3 1.0 %copy-start = (f32[16,8,8,128]{3,2,1,0:T(8,128)S(1)}, f32[16,8,8,128]{3,2,1,0:T(8,128)}, u32[]{:S(2)}) copy-start(f32[16,8,8,128]{3,2,1,0:T(8,128)} %refs_0_.1) | copy-start | bytes 1572868
  2.3 0.8 %copy-start.1 = (f32[8,8,128]{2,1,0:T(8,128)S(1)}, f32[8,8,128]{2,1,0:T(8,128)}, u32[]{:S(2)}) copy-start(f32[8,8,128]{2,1,0:T(8,128)} %refs_1_.1) | copy-start | bytes 98308
  3.1 0.7 %copy-start.2 = (s32[4,3,384]{2,0,1:T(4,128)S(1)}, s32[4,3,384]{2,0,1:T(4,128)}, u32[]{:S(2)}) copy-start(s32[4,3,384]{2,0,1:T(4,128)} %param.13) | copy-start | bytes 55300
  3.8 0.7 copy-start.3
  4.5 0.7 copy-start.4
  5.2 0.7 copy-start.5
  5.8 0.7 copy-start.6

commit v2 on v1

--- a/solution.py
+++ b/solution.py
@@ -176,8 +176,8 @@
             top = float(np.float32(ml_dtypes.bfloat16(weight)))
             high = jnp.where(distance == reach, top, high)
             low = jnp.where(distance == reach, weight - top, low)
-        matrices[2 * which] = high.astype(jnp.bfloat16)
-        matrices[2 * which + 1] = low.astype(jnp.bfloat16)
+        for place, part in enumerate((high, high, low)):
+            matrices[which, pl.ds(place * size, size)] = part.astype(jnp.bfloat16)
 
 
 def split_three(value):
@@ -189,7 +189,7 @@
 def build_tables(offsets, beta, tables):
     points = beta.shape[1]
     for kind in range(beta.shape[0]):
-        dx, dy, dz = (offsets[axis, kind : kind + 1, :] + 5 for axis in range(3))
+        dx, dy, dz = (offsets[kind, axis : axis + 1, :] + 5 for axis in range(3))
         parts = split_three(beta[kind : kind + 1, :])
         for phase in range(per_group):
             moved = dx + phase
@@ -318,30 +318,25 @@
         copy.wait()
 
 
-def plane_part(source, matrices, plane, high, low, window):
+def plane_part(source, matrices, plane, split, window):
     inner = pl.ds(low_rows, window)
     for tile in range(groups // 2):
         wide = jnp.concatenate(
             [source[low_groups + 2 * tile, inner], source[low_groups + 2 * tile + 1, inner]], axis=1
         )
         big = wide.astype(jnp.bfloat16)
-        high[pl.ds(tile * window, window)] = big
-        low[pl.ds(tile * window, window)] = (wide - big.astype(jnp.float32)).astype(jnp.bfloat16)
+        rows = pl.ds(tile * window, window)
+        split[rows, : 2 * lanes] = big
+        split[rows, 2 * lanes : 4 * lanes] = (wide - big.astype(jnp.float32)).astype(jnp.bfloat16)
+        split[rows, 4 * lanes :] = big
     total = groups // 2 * window
 
-    def product(part, which, begin, end):
-        return jnp.dot(part[begin:end], matrices[which], preferred_element_type=jnp.float32)
-
-    def triple(which, begin, end):
-        return (
-            product(high, which, begin, end)
-            + product(low, which, begin, end)
-            + product(high, which + 1, begin, end)
-        )
-
-    plane[...] = triple(0, 0, total)
-    plane[window:] += triple(2, 0, total - window)
-    plane[: total - window] += triple(4, window, total)
+    def product(which, begin, end):
+        return jnp.dot(split[begin:end], matrices[which], preferred_element_type=jnp.float32)
+
+    plane[...] = product(0, 0, total)
+    plane[window:] += product(1, 0, total - window)
+    plane[: total - window] += product(2, window, total)
 
 
 def local_part(source, potential, plane, part, half, window):
@@ -361,7 +356,7 @@
 
 def filter_kernel(
     depth, atoms, field, potential, tables, matrices, strengths, ping, pong,
-    plane, high, low, shapes, listed, found,
+    plane, split, shapes, listed, found,
 ):
     window = field.shape[1]
     slots = 8
@@ -440,7 +435,7 @@
         scatter(target, batches - 1, gains)
 
     def step(source, target, scale, keep):
-        plane_part(source, matrices, plane, high, low, window)
+        plane_part(source, matrices, plane, split, window)
         for part in range(groups // 2):
             for half in range(2):
                 padded = low_groups + 2 * part + half
@@ -460,7 +455,7 @@
 
 def collect_kernel(
     shape, cells, source, rest, potential, matrices, block, gram,
-    plane, high, low, turning, pieces, partial, sums, local_sem, send_sem, recv_sem, sum_send, sum_recv,
+    plane, split, turning, pieces, partial, sums, local_sem, send_sem, recv_sem, sum_send, sum_recv,
 ):
     slabs, rows, cols = shape
     bands, _, _, depth = block.shape
@@ -477,7 +472,7 @@
     barrier = pltpu.get_barrier_semaphore()
     for step in range(1, devices):
         pl.semaphore_signal(barrier, inc=1, device_id=partner(step), device_id_type=MESH)
-    plane_part(source, matrices, plane, high, low, window)
+    plane_part(source, matrices, plane, split, window)
     begin = pl.multiple_of(col * margin, margin)
     copies = []
     for order, s in enumerate((1, 2, 3, 0)):
@@ -572,7 +567,7 @@
     hbm = pl.BlockSpec(memory_space=pltpu.HBM)
     dma = pltpu.SemaphoreType.DMA
     table_count = beta.shape[0] * per_group
-    matrices_shape = jax.ShapeDtypeStruct((6, 2 * lanes, 2 * lanes), jnp.bfloat16)
+    matrices_shape = jax.ShapeDtypeStruct((3, 6 * lanes, 2 * lanes), jnp.bfloat16)
     field, wide_potential, atoms, tables, matrices, strengths = pl.pallas_call(
         lambda *refs: spread_kernel(shape, *refs),
         out_shape=(
@@ -600,14 +595,13 @@
             collective_id=0, has_side_effects=True, vmem_limit_bytes=32 * 2**20
         ),
         name="spread",
-    )(wave, potential, positions, species, counts, offsets.transpose(1, 0, 2), beta, coupling)
+    )(wave, potential, positions, species, counts, offsets, beta, coupling)
 
     most = bands * cols * slots + unroll
     padded = jax.ShapeDtypeStruct((groups + 2 * low_groups, window + 2 * low_rows, lanes), jnp.float32)
     plane_scratch = [
         pltpu.VMEM((groups // 2 * window, 2 * lanes), jnp.float32),
-        pltpu.VMEM((groups // 2 * window, 2 * lanes), jnp.bfloat16),
-        pltpu.VMEM((groups // 2 * window, 2 * lanes), jnp.bfloat16),
+        pltpu.VMEM((groups // 2 * window, 6 * lanes), jnp.bfloat16),
     ]
     second, rest = pl.pallas_call(
         lambda *refs: filter_kernel(size_z, *refs),

time: 70.4 us -> 70.8 us (level); the launches traced: 70 us -> 71.5 us
  Pallas kernels: 62.1 us -> 63.6 us
    pallas_call x1, Pallas kernels: 14.8 us -> 16.3 us  [band_shards(): pl.pallas_call(lambda *refs: filter_kernel(size_z, *refs), out_shape=(pad...]
    unnamed x16 -> x15, local copies, waits for them, and re-layouts: 6.59 us -> 6.6 us
where the time goes in v2:
time: 70.8 us; the launch traced here: 71.5 us
  Pallas kernels  63.6 us (90%)
  local copies, waits for them, and re-layouts  6.6 us (9%)
  between operations  1.31 us (2%)
    pallas_call x1, Pallas kernels, band_shards(): pl.pallas_call(lambda *refs: spread_kernel(shape, *refs), out_shape=(jax....  23.9 us
    pallas_call x1, Pallas kernels, band_shards(): pl.pallas_call(lambda *refs: collect_kernel(shape, cells, *refs), out_sha...  23.5 us
    pallas_call x1, Pallas kernels, band_shards(): pl.pallas_call(lambda *refs: filter_kernel(size_z, *refs), out_shape=(pad...  16.3 us
    unnamed x15, local copies, waits for them, and re-layouts  6.6 us

profile of v2, /device:TPU:0, one launch (start us, length us, event | category | flops | bytes accessed | tf_op | source)
XLA Modules:
  0.0 71.5 jit_solution(6695575632968391665)
XLA Ops:
  1.3 0.7 %copy.10.refs_5_ = s32[4,3,384]{2,1,0:T(4,128)S(1)} copy(s32[4,3,384]{2,0,1:T(4,128)} %param.13) | data formatting | bytes 36864 | tf_op args[5]
  2.0 0.0 copy-start
  2.0 1.0 %copy-done = f32[16,8,8,128]{3,2,1,0:T(8,128)S(1)} copy-done((f32[16,8,8,128]{3,2,1,0:T(8,128)S(1)}, f32[16,8,8,128]{3,2,1,0:T(8,128)}, u32[]{:S(2)}) %copy-start) | copy-done | bytes 524312
  3.0 0.0 copy-start.1
  3.1 0.8 %copy-done.1 = f32[8,8,128]{2,1,0:T(8,128)S(1)} copy-done((f32[8,8,128]{2,1,0:T(8,128)S(1)}, f32[8,8,128]{2,1,0:T(8,128)}, u32[]{:S(2)}) %copy-start.1) | copy-done | bytes 32792
  3.8 0.0 copy-start.2
  3.8 0.7 copy-done.2
  4.5 0.0 copy-start.3
  4.5 0.7 copy-done.3
  5.2 0.0 copy-start.4
  5.2 0.7 copy-done.4
  5.8 0.0 copy-start.5
  5.8 0.7 copy-done.5
  6.5 23.9 %spread.1 = (f32[8,160,128]{2,1,0:T(8,128)S(1)}, f32[8,160,128]{2,1,0:T(8,128)S(1)}, s32[2,16,1,128]{3,2,1,0:T(1,128)S(1)}, f32[16,64,128]{2,1,0:T(8,128)S(1)}, ...) custom-call(f32[16,8,8,128]{3,2,1,0:T(8,128)S(1)} %copy-done, f32[8,8,128]{2,1,0:T(8,128)S(1)} %copy-done.1, ...), custom_call_target="tpu_custom_call" | custom-call | tf_op jit(solution)/shard_map/spread/pallas_call | solution.py:571
  30.4 16.3 %chebyshev.1 = (f32[12,192,128]{2,1,0:T(8,128)S(1)}, f32[12,192,128]{2,1,0:T(8,128)S(1)}) custom-call(s32[32,1,128]{2,1,0:T(1,128)S(1)} %bitcast.1, f32[8,160,128]{2,1,0:T(8,128)S(1)} %get-tuple-element.11.refs_1_, f32[8,160,128]{2,1,0:T(8,128)S(1)} %get-tuple-element.12.refs_2_, f32[16,64,128]{2,1,0:T(8,128)S(1)} %get-tuple-element.13.refs_3_, ...), custom_call_target="tpu_custom_call" | custom-call | tf_op jit(solution)/shard_map/chebyshev/pallas_call | solution.py:606
  46.6 23.5 %collect.1 = (f32[16,8,8,128]{3,2,1,0:T(8,128)S(1)}, f32[16,16]{1,0:T(8,128)S(1)}) custom-call(f32[12,192,128]{2,1,0:T(8,128)S(1)} %get-tuple-element.16.refs_0_, f32[12,192,128]{2,1,0:T(8,128)S(1)} %get-tuple-element.17.refs_1_, f32[8,160,128]{2,1,0:T(8,128)S(1)} %get-tuple-element.12.refs_2_, bf16[3,768,256]{2,1,0:T(8,128)(2,1)S(1)} %get-tuple-element.14.refs_4_.refs_3_), custom_call_target="tpu_custom_call" | custom-call | tf_op jit(solution)/shard_map/collect/pallas_call | solution.py:623
  70.1 0.8 %copy.14 = f32[16,8,8,128]{3,2,1,0:T(8,128)} copy(f32[16,8,8,128]{3,2,1,0:T(8,128)S(1)} %get-tuple-element.20) | data formatting | bytes 1048576
  70.9 0.6 copy.15
Async XLA Ops:
  2.0 1.0 %copy-start = (f32[16,8,8,128]{3,2,1,0:T(8,128)S(1)}, f32[16,8,8,128]{3,2,1,0:T(8,128)}, u32[]{:S(2)}) copy-start(f32[16,8,8,128]{3,2,1,0:T(8,128)} %refs_0_.1) | copy-start | bytes 1572868
  3.0 0.8 %copy-start.1 = (f32[8,8,128]{2,1,0:T(8,128)S(1)}, f32[8,8,128]{2,1,0:T(8,128)}, u32[]{:S(2)}) copy-start(f32[8,8,128]{2,1,0:T(8,128)} %refs_1_.1) | copy-start | bytes 98308
  3.8 0.7 copy-start.2
  4.5 0.7 copy-start.3
  5.2 0.7 copy-start.4
  5.8 0.7 copy-start.5

commit v3 on v1

--- a/solution.py
+++ b/solution.py
@@ -210,8 +210,9 @@
 
 
 def spread_kernel(
-    shape, wave, potential, positions, species, counts, offsets, beta, coupling,
-    field_out, potential_out, atoms_out, tables, matrices, strengths, got, info, local_sem, send_sem, recv_sem, part_send, part_recv, pair_send, pair_recv,
+    shape, wave, potential, positions_in, species_in, counts, offsets_in, beta_in, coupling_in,
+    field_out, potential_out, atoms_out, tables, matrices, strengths,
+    positions, species, offsets, beta, coupling, small_sem, got, info, local_sem, send_sem, recv_sem, part_send, part_recv, pair_send, pair_recv,
 ):
     slabs, rows, _ = shape
     depth = wave.shape[3]
@@ -223,12 +224,24 @@
     def partner(shift):
         return (lax.rem(slab + shift[0], slabs), lax.rem(row + shift[1], rows), col)
 
+    small = (
+        (positions_in, positions),
+        (species_in, species),
+        (offsets_in, offsets),
+        (beta_in, beta),
+        (coupling_in, coupling),
+    )
+    small = [pltpu.make_async_copy(*pair, small_sem.at[index]) for index, pair in enumerate(small)]
+    for copy in small:
+        copy.start()
     barrier = pltpu.get_barrier_semaphore()
     for shift in shifts:
         if shift != (0, 0):
             pl.semaphore_signal(barrier, inc=1, device_id=partner(shift), device_id_type=MESH)
     pl.semaphore_signal(barrier, inc=1, device_id=other, device_id_type=MESH)
 
+    for copy in small:
+        copy.wait()
     slots = positions.shape[1]
     live = (lax.broadcasted_iota(jnp.int32, (1, slots), 1) < counts[0]).astype(jnp.int32)
     words = [positions[0:1, :], positions[1:2, :], positions[2:3, :], species[...].reshape(1, slots), live]
@@ -573,6 +586,9 @@
     dma = pltpu.SemaphoreType.DMA
     table_count = beta.shape[0] * per_group
     matrices_shape = jax.ShapeDtypeStruct((6, 2 * lanes, 2 * lanes), jnp.bfloat16)
+    offsets = offsets.transpose(1, 0, 2)
+    held = (wave, potential, positions, species, counts, offsets, beta, coupling)
+    held = [a if a is counts else pltpu.with_memory_space_constraint(a, pltpu.HBM) for a in held]
     field, wide_potential, atoms, tables, matrices, strengths = pl.pallas_call(
         lambda *refs: spread_kernel(shape, *refs),
         out_shape=(
@@ -583,9 +599,15 @@
             matrices_shape,
             jax.ShapeDtypeStruct((beta.shape[0] + 1, 1, lanes), jnp.float32),
         ),
-        in_specs=[hbm, hbm, vmem, vmem, smem, vmem, vmem, smem],
+        in_specs=[hbm] * 4 + [smem] + [hbm] * 3,
         out_specs=[vmem] * 6,
         scratch_shapes=[
+            pltpu.VMEM(positions.shape, jnp.int32),
+            pltpu.VMEM(species.shape, jnp.int32),
+            pltpu.VMEM(offsets.shape, jnp.int32),
+            pltpu.VMEM(beta.shape, jnp.float32),
+            pltpu.SMEM(coupling.shape, jnp.float32),
+            dma((5,)),
             pltpu.VMEM((2, bands, size_x, size_y, size_z), jnp.float32),
             pltpu.VMEM((1, lanes), jnp.int32),
             dma((3,)),
@@ -600,7 +622,7 @@
             collective_id=0, has_side_effects=True, vmem_limit_bytes=32 * 2**20
         ),
         name="spread",
-    )(wave, potential, positions, species, counts, offsets.transpose(1, 0, 2), beta, coupling)
+    )(*held)
 
     most = bands * cols * slots + unroll
     padded = jax.ShapeDtypeStruct((groups + 2 * low_groups, window + 2 * low_rows, lanes), jnp.float32)

time: 70.4 us -> 64.8 us (0.920)
  local copies, waits for them, and re-layouts: 6.59 us -> 1.39 us
  Pallas kernels: 62.1 us -> 61.2 us
    unnamed x16 -> x2, local copies, waits for them, and re-layouts: 6.59 us -> 1.39 us
where the time goes in v3:
time: 64.8 us; the launch traced here: 63.9 us
  Pallas kernels  61.2 us (94%)
  local copies, waits for them, and re-layouts  1.39 us (2%)
  between operations  1.3 us (2%)
    pallas_call x1, Pallas kernels, band_shards(): pl.pallas_call(lambda *refs: spread_kernel(shape, *refs), out_shape=(jax....  23.6 us
    pallas_call x1, Pallas kernels, band_shards(): pl.pallas_call(lambda *refs: collect_kernel(shape, cells, *refs), out_sha...  23.5 us
    pallas_call x1, Pallas kernels, band_shards(): pl.pallas_call(lambda *refs: filter_kernel(size_z, *refs), out_shape=(pad...  14.1 us
    unnamed x2, local copies, waits for them, and re-layouts  1.39 us

profile of v3, /device:TPU:0, one launch (start us, length us, event | category | flops | bytes accessed | tf_op | source)
XLA Modules:
  0.0 63.9 jit_solution(16539947214818504527)
XLA Ops:
  1.3 23.6 %spread.1 = (f32[8,160,128]{2,1,0:T(8,128)S(1)}, f32[8,160,128]{2,1,0:T(8,128)S(1)}, s32[2,16,1,128]{3,2,1,0:T(1,128)S(1)}, f32[16,64,128]{2,1,0:T(8,128)S(1)}, ...) custom-call(f32[16,8,8,128]{3,2,1,0:T(8,128)} %refs_0_.1, f32[8,8,128]{2,1,0:T(8,128)} %refs_1_.1, ...), custom_call_target="tpu_custom_call" | custom-call | tf_op jit(solution)/shard_map/spread/pallas_call | solution.py:592
  24.9 14.1 %chebyshev.1 = (f32[12,192,128]{2,1,0:T(8,128)S(1)}, f32[12,192,128]{2,1,0:T(8,128)S(1)}) custom-call(s32[32,1,128]{2,1,0:T(1,128)S(1)} %bitcast.2, f32[8,160,128]{2,1,0:T(8,128)S(1)} %get-tuple-element.11.refs_1_, f32[8,160,128]{2,1,0:T(8,128)S(1)} %get-tuple-element.12.refs_2_, f32[16,64,128]{2,1,0:T(8,128)S(1)} %get-tuple-element.13.refs_3_, ...), custom_call_target="tpu_custom_call" | custom-call | tf_op jit(solution)/shard_map/chebyshev/pallas_call | solution.py:634
  39.0 23.5 %collect.1 = (f32[16,8,8,128]{3,2,1,0:T(8,128)S(1)}, f32[16,16]{1,0:T(8,128)S(1)}) custom-call(f32[12,192,128]{2,1,0:T(8,128)S(1)} %get-tuple-element.16.refs_0_, f32[12,192,128]{2,1,0:T(8,128)S(1)} %get-tuple-element.17.refs_1_, f32[8,160,128]{2,1,0:T(8,128)S(1)} %get-tuple-element.12.refs_2_, bf16[6,256,256]{2,1,0:T(8,128)(2,1)S(1)} %get-tuple-element.14.refs_4_.refs_3_), custom_call_target="tpu_custom_call" | custom-call | tf_op jit(solution)/shard_map/collect/pallas_call | solution.py:651
  62.5 0.8 %copy.13 = f32[16,8,8,128]{3,2,1,0:T(8,128)} copy(f32[16,8,8,128]{3,2,1,0:T(8,128)S(1)} %get-tuple-element.20) | data formatting | bytes 1048576
  63.3 0.6 copy.14

commit v4 on v3

--- a/solution.py
+++ b/solution.py
@@ -402,7 +402,55 @@
             count = count + jnp.where((local >= -5) & (local <= window + 4), live, 0)
         return count
 
-    count = lax.fori_loop(0, atoms.shape[0], find, jnp.int32(0))
+    def gather(source, index, scale):
+        gains = []
+        for extra in range(unroll):
+            atom = index * unroll + extra
+            group, at = found[0, atom], found[1, atom]
+            total = jnp.zeros((box, lanes), jnp.float32)
+            for part in range(4):
+                total = total + source[group + part, pl.ds(at, box)] * shapes[atom, pl.ds(part * box, box)]
+            summed = jnp.sum(jnp.sum(total, axis=0, keepdims=True), axis=1, keepdims=True)
+            gains.append(summed * (strengths[found[2, atom]] * scale))
+        return tuple(gains)
+
+    def scatter(target, index, gains):
+        for extra in range(unroll):
+            atom = index * unroll + extra
+            group, at = found[0, atom], found[1, atom]
+            for part in range(4):
+                target[group + part, pl.ds(at, box)] += gains[extra] * shapes[atom, pl.ds(part * box, box)]
+
+    def project(source, target, scale):
+        def batch(index, gains):
+            later = gather(source, index, scale)
+            scatter(target, index - 1, gains)
+            return later
+
+        gains = lax.fori_loop(1, batches, batch, gather(source, 0, scale))
+        scatter(target, batches - 1, gains)
+
+    def stencil_step(source, target, scale, keep, between=None):
+        plane_part(source, matrices, plane, high, low, window)
+        for part in range(groups // 2):
+            for half in range(2):
+                padded = low_groups + 2 * part + half
+                value = local_part(source, potential, plane, part, half, window)
+                if keep:
+                    value = scale * value - target[padded, inner]
+                target[padded, inner] = value
+                if between is not None:
+                    between(2 * part + half)
+
+    counts = [jnp.int32(0)]
+    share = atoms.shape[0] // groups
+
+    def find_some(index):
+        for block in range(index * share, (index + 1) * share):
+            counts.append(find(block, counts[-1]))
+
+    stencil_step(ping, pong, 1.0, False, find_some)
+    count = counts[-1]
     for extra in range(unroll):
         listed[count + extra] = 0
     batches = jnp.maximum((count + unroll - 1) // unroll, 1)
@@ -424,48 +472,11 @@
 
     lax.fori_loop(0, batches, shape_batch, 0)
 
-    def gather(source, index, scale):
-        gains = []
-        for extra in range(unroll):
-            atom = index * unroll + extra
-            group, at = found[0, atom], found[1, atom]
-            total = jnp.zeros((box, lanes), jnp.float32)
-            for part in range(4):
-                total = total + source[group + part, pl.ds(at, box)] * shapes[atom, pl.ds(part * box, box)]
-            summed = jnp.sum(jnp.sum(total, axis=0, keepdims=True), axis=1, keepdims=True)
-            gains.append(summed * (strengths[found[2, atom]] * scale))
-        return tuple(gains)
-
-    def scatter(target, index, gains):
-        for extra in range(unroll):
-            atom = index * unroll + extra
-            group, at = found[0, atom], found[1, atom]
-            for part in range(4):
-                target[group + part, pl.ds(at, box)] += gains[extra] * shapes[atom, pl.ds(part * box, box)]
-
-    def project(source, target, scale):
-        def batch(index, gains):
-            later = gather(source, index, scale)
-            scatter(target, index - 1, gains)
-            return later
-
-        gains = lax.fori_loop(1, batches, batch, gather(source, 0, scale))
-        scatter(target, batches - 1, gains)
-
-    def step(source, target, scale, keep):
-        plane_part(source, matrices, plane, high, low, window)
-        for part in range(groups // 2):
-            for half in range(2):
-                padded = low_groups + 2 * part + half
-                value = local_part(source, potential, plane, part, half, window)
-                if keep:
-                    value = scale * value - target[padded, inner]
-                target[padded, inner] = value
-        project(source, target, scale)
-        clear_rims(target)
-
-    step(ping, pong, 1.0, False)
-    step(pong, ping, 2.0, True)
+    project(ping, pong, 1.0)
+    clear_rims(pong)
+    stencil_step(pong, ping, 2.0, True)
+    project(pong, ping, 2.0)
+    clear_rims(ping)
     middle = pl.ds(low_groups, groups)
     pong[middle, inner] = -pong[middle, inner]
     project(ping, pong, 2.0)
@@ -473,7 +484,7 @@
 
 def collect_kernel(
     shape, cells, source, rest, potential, matrices, block, gram,
-    plane, high, low, turning, pieces, partial, sums, local_sem, send_sem, recv_sem, sum_send, sum_recv,
+    plane, high, low, turning, pieces, gram_high, gram_low, partial, sums, local_sem, send_sem, recv_sem, sum_send, sum_recv,
 ):
     slabs, rows, cols = shape
     bands, _, _, depth = block.shape
@@ -523,17 +534,22 @@
                     )
                 )
             copies[-1].start()
-    for copy in copies:
-        copy.wait()
-
     size_x, size_y = block.shape[1:3]
     flat = bands * size_y
-    wide = jnp.concatenate([block[:, x].reshape(flat, lanes) for x in range(size_x)], axis=1)
-    high = wide.astype(jnp.bfloat16)
-    low = (wide - high.astype(jnp.float32)).astype(jnp.bfloat16)
+    some = rows * size_y
+    for order, s in enumerate((1, 2, 3, 0)):
+        for copy in copies[order * rows : (order + 1) * rows]:
+            copy.wait()
+        part = lax.rem(slab + (slabs - s), slabs)
+        at = pl.ds(pl.multiple_of(part * some, some), some)
+        for x in range(size_x):
+            value = block[pl.ds(part * rows, rows), x].reshape(some, lanes)
+            big = value.astype(jnp.bfloat16)
+            gram_high[at, x * lanes : (x + 1) * lanes] = big
+            gram_low[at, x * lanes : (x + 1) * lanes] = (value - big.astype(jnp.float32)).astype(jnp.bfloat16)
     product = lax.dot_general(
-        high,
-        jnp.concatenate([high, low], axis=0),
+        gram_high[...],
+        jnp.concatenate([gram_high[...], gram_low[...]], axis=0),
         (((1,), (1,)), ((), ())),
         preferred_element_type=jnp.float32,
     )
@@ -660,6 +676,8 @@
         + [
             pltpu.VMEM((2, window, lanes), jnp.float32),
             pltpu.VMEM(wave.shape, jnp.float32),
+            pltpu.VMEM((bands * size_y, size_x * lanes), jnp.bfloat16),
+            pltpu.VMEM((bands * size_y, size_x * lanes), jnp.bfloat16),
             pltpu.VMEM((2, lanes), jnp.float32),
             pltpu.VMEM((devices, 2, lanes), jnp.float32),
             dma,

time: 64.8 us -> 64.1 us (0.989)
  no operation moved by 1% of the time
where the time goes in v4:
time: 64.1 us; the launch traced here: 63.5 us
  Pallas kernels  60.8 us (95%)
  local copies, waits for them, and re-layouts  1.39 us (2%)
  between operations  1.29 us (2%)
    pallas_call x1, Pallas kernels, band_shards(): pl.pallas_call(lambda *refs: spread_kernel(shape, *refs), out_shape=(jax....  23.6 us
    pallas_call x1, Pallas kernels, band_shards(): pl.pallas_call(lambda *refs: collect_kernel(shape, cells, *refs), out_sha...  23.5 us
    pallas_call x1, Pallas kernels, band_shards(): pl.pallas_call(lambda *refs: filter_kernel(size_z, *refs), out_shape=(pad...  13.7 us
    unnamed x2, local copies, waits for them, and re-layouts  1.39 us

profile of v4, /device:TPU:0, one launch (start us, length us, event | category | flops | bytes accessed | tf_op | source)
XLA Modules:
  0.0 63.5 jit_solution(4047567009124707841)
XLA Ops:
  1.3 23.6 %spread.1 = (f32[8,160,128]{2,1,0:T(8,128)S(1)}, f32[8,160,128]{2,1,0:T(8,128)S(1)}, s32[2,16,1,128]{3,2,1,0:T(1,128)S(1)}, f32[16,64,128]{2,1,0:T(8,128)S(1)}, ...) custom-call(f32[16,8,8,128]{3,2,1,0:T(8,128)} %refs_0_.1, f32[8,8,128]{2,1,0:T(8,128)} %refs_1_.1, ...), custom_call_target="tpu_custom_call" | custom-call | tf_op jit(solution)/shard_map/spread/pallas_call | solution.py:608
  24.9 13.7 %chebyshev.1 = (f32[12,192,128]{2,1,0:T(8,128)S(1)}, f32[12,192,128]{2,1,0:T(8,128)S(1)}) custom-call(s32[32,1,128]{2,1,0:T(1,128)S(1)} %bitcast.2, f32[8,160,128]{2,1,0:T(8,128)S(1)} %get-tuple-element.11.refs_1_, f32[8,160,128]{2,1,0:T(8,128)S(1)} %get-tuple-element.12.refs_2_, f32[16,64,128]{2,1,0:T(8,128)S(1)} %get-tuple-element.13.refs_3_, ...), custom_call_target="tpu_custom_call" | custom-call | tf_op jit(solution)/shard_map/chebyshev/pallas_call | solution.py:650
  38.6 23.5 %collect.1 = (f32[16,8,8,128]{3,2,1,0:T(8,128)S(1)}, f32[16,16]{1,0:T(8,128)S(1)}) custom-call(f32[12,192,128]{2,1,0:T(8,128)S(1)} %get-tuple-element.16.refs_0_, f32[12,192,128]{2,1,0:T(8,128)S(1)} %get-tuple-element.17.refs_1_, f32[8,160,128]{2,1,0:T(8,128)S(1)} %get-tuple-element.12.refs_2_, bf16[6,256,256]{2,1,0:T(8,128)(2,1)S(1)} %get-tuple-element.14.refs_4_.refs_3_), custom_call_target="tpu_custom_call" | custom-call | tf_op jit(solution)/shard_map/collect/pallas_call | solution.py:667
  62.1 0.8 %copy.13 = f32[16,8,8,128]{3,2,1,0:T(8,128)} copy(f32[16,8,8,128]{3,2,1,0:T(8,128)S(1)} %get-tuple-element.20) | data formatting | bytes 1048576
  62.9 0.6 copy.14

commit v5 on v4

--- a/solution.py
+++ b/solution.py
@@ -154,7 +154,7 @@
 low_groups = 2
 low_rows = 16
 box = 16
-unroll = 8
+unroll = 16
 centre = 0.5 * (upper_edge + lower_edge)
 half_width = 0.5 * (upper_edge - lower_edge)
 MESH = pl.DeviceIdType.MESH

time: 64.1 us -> 61.4 us (0.958)
  Pallas kernels: 60.8 us -> 58.5 us
    pallas_call x1, Pallas kernels: 13.7 us -> 11.3 us  [band_shards(): pl.pallas_call(lambda *refs: filter_kernel(size_z, *refs), out_shape=(pad...]
where the time goes in v5:
time: 61.4 us; the launch traced here: 61.2 us
  Pallas kernels  58.5 us (95%)
  local copies, waits for them, and re-layouts  1.39 us (2%)
  between operations  1.3 us (2%)
    pallas_call x1, Pallas kernels, band_shards(): pl.pallas_call(lambda *refs: spread_kernel(shape, *refs), out_shape=(jax....  23.6 us
    pallas_call x1, Pallas kernels, band_shards(): pl.pallas_call(lambda *refs: collect_kernel(shape, cells, *refs), out_sha...  23.5 us
    pallas_call x1, Pallas kernels, band_shards(): pl.pallas_call(lambda *refs: filter_kernel(size_z, *refs), out_shape=(pad...  11.3 us
    unnamed x2, local copies, waits for them, and re-layouts  1.39 us

profile of v5, /device:TPU:0, one launch (start us, length us, event | category | flops | bytes accessed | tf_op | source)
XLA Modules:
  0.0 61.2 jit_solution(7626188068054654306)
XLA Ops:
  1.3 23.6 %spread.1 = (f32[8,160,128]{2,1,0:T(8,128)S(1)}, f32[8,160,128]{2,1,0:T(8,128)S(1)}, s32[2,16,1,128]{3,2,1,0:T(1,128)S(1)}, f32[16,64,128]{2,1,0:T(8,128)S(1)}, ...) custom-call(f32[16,8,8,128]{3,2,1,0:T(8,128)} %refs_0_.1, f32[8,8,128]{2,1,0:T(8,128)} %refs_1_.1, ...), custom_call_target="tpu_custom_call" | custom-call | tf_op jit(solution)/shard_map/spread/pallas_call | solution.py:608
  24.9 11.3 %chebyshev.1 = (f32[12,192,128]{2,1,0:T(8,128)S(1)}, f32[12,192,128]{2,1,0:T(8,128)S(1)}) custom-call(s32[32,1,128]{2,1,0:T(1,128)S(1)} %bitcast.2, f32[8,160,128]{2,1,0:T(8,128)S(1)} %get-tuple-element.11.refs_1_, f32[8,160,128]{2,1,0:T(8,128)S(1)} %get-tuple-element.12.refs_2_, f32[16,64,128]{2,1,0:T(8,128)S(1)} %get-tuple-element.13.refs_3_, ...), custom_call_target="tpu_custom_call" | custom-call | tf_op jit(solution)/shard_map/chebyshev/pallas_call | solution.py:650
  36.3 23.5 %collect.1 = (f32[16,8,8,128]{3,2,1,0:T(8,128)S(1)}, f32[16,16]{1,0:T(8,128)S(1)}) custom-call(f32[12,192,128]{2,1,0:T(8,128)S(1)} %get-tuple-element.16.refs_0_, f32[12,192,128]{2,1,0:T(8,128)S(1)} %get-tuple-element.17.refs_1_, f32[8,160,128]{2,1,0:T(8,128)S(1)} %get-tuple-element.12.refs_2_, bf16[6,256,256]{2,1,0:T(8,128)(2,1)S(1)} %get-tuple-element.14.refs_4_.refs_3_), custom_call_target="tpu_custom_call" | custom-call | tf_op jit(solution)/shard_map/collect/pallas_call | solution.py:667
  59.8 0.8 %copy.13 = f32[16,8,8,128]{3,2,1,0:T(8,128)} copy(f32[16,8,8,128]{3,2,1,0:T(8,128)S(1)} %get-tuple-element.20) | data formatting | bytes 1048576
  60.6 0.6 copy.14
